TPU v7x, 512 devices: a whole 4x8x8 slice. The times are simulated.
512 devices in a mesh: seq: 128 (over z, y, core), mp: 2 (over x_lo), dp: 2 (over x_hi).
Axes of the slice: x: 4 (x_hi: 2, x_lo: 2; x = x_hi * 2 + x_lo), y: 8, z: 8, core: 2. Of those that a mesh axis runs over, the one named last changes fastest.
Arguments:
- byte_rows: bfloat16 [65536, 1280], P(('dp', 'seq')), parts along dimension 0, may hold values from -6 to 6
- norm_gain: float32 [1280], replicated, may hold values from 0.1 to 1.9
- key_weight: bfloat16 [1280, 512], P('seq', 'mp'), may hold values from -0.15625 to 0.15625
- value_weight: bfloat16 [1280, 3072], P('seq', 'mp'), may hold values from -0.15625 to 0.15625
- pool_query: float32 [4, 128], P('mp'), may hold values from -320 to 320
- patch_starts: int32 [8192], P(('dp', 'seq')), parts along dimension 0, may hold values from 0 to 32767, as said below
Outputs:
- patch_mix: bfloat16 [8192, 2048], P(('dp', 'seq'), 'mp'), parts along dimension 0
There are 2 independent parts, one for each index of `dp`. A program takes and returns all parts, laid end to end along the dimension named above; an argument that names none is the same for every part. Nothing has to cross between parts.
Inputs may be any that keep to these rules, and one draw needn't show every extreme that they name: Sorted and distinct. The bytes fall into aligned blocks of 1024 bytes (the bytes of 4 neighbouring indices of seq, starting at index 0); each block holds exactly 128 patches, the first starting at the block's first byte. Patch p covers the bytes from patch_starts[p] to the next start minus 1 (the last patch to 32767). No patch is longer than 256 bytes, and each block holds a patch of exactly 256 bytes.
All inputs are finite; a program needn't handle non-finite values.
Results may differ from a plain program's by a relative error of at most 0.014.
Values may be sent and summed in bfloat16 or wider, within the bound.
A program may use at most 64 MiB of HBM per device.

v0:
```python
import math

import jax
import jax.numpy as jnp
from jax import lax
from jax.sharding import PartitionSpec as P

DH = 128
GQ = 4


def partner(block, axis, distance):
    count = lax.axis_size(axis)
    route = []
    for low in range(count):
        high = low | 1 << distance
        if high != low and high < count:
            route += [(low, high), (high, low)]
    return lax.ppermute(block, axis, route)


def on_device(byte_rows, norm_gain, key_weight, value_weight, pool_query, patch_starts):
    byte_count = byte_rows.shape[0]
    patch_count = patch_starts.shape[0]
    block_patches = 4 * patch_count
    local_heads = pool_query.shape[0]
    device_index = lax.axis_index("seq")
    block_position = device_index % 4
    widened = byte_rows.astype(jnp.float32)
    scale_row = lax.rsqrt(jnp.mean(widened * widened, axis=-1, keepdims=True) + 1e-05)
    normed = (widened * scale_row * norm_gain).astype(jnp.bfloat16)
    block_starts = patch_starts
    for which_bit in range(2):
        partner_starts = partner(block_starts, "seq", which_bit)
        upper_side = block_position // (1 << which_bit) % 2
        block_starts = jnp.where(
            upper_side == 1,
            jnp.concatenate([partner_starts, block_starts]),
            jnp.concatenate([block_starts, partner_starts]),
        )
    positions = device_index * byte_count + jnp.arange(byte_count, dtype=jnp.int32)
    segment = jnp.sum((block_starts[:, None] <= positions[None, :]).astype(jnp.int32), axis=0) - 1
    member = segment[None, :] == jnp.arange(block_patches, dtype=jnp.int32)[:, None]
    full_keys, full_values = (
        lax.all_gather(key_weight, "seq", axis=0, tiled=True),
        lax.all_gather(value_weight, "seq", axis=0, tiled=True),
    )
    byte_keys = jnp.dot(normed, full_keys, preferred_element_type=jnp.float32)
    byte_values = jnp.dot(normed, full_values, preferred_element_type=jnp.float32).astype(
        jnp.bfloat16
    )
    head_keys = byte_keys.reshape(byte_count, local_heads, DH)
    pool_scores = jnp.einsum(
        "bgd,gd->bg", head_keys, pool_query, precision=lax.Precision.HIGHEST
    ) / math.sqrt(DH)
    masked = jnp.where(member[:, :, None], pool_scores[None, :, :], -1e30)
    patch_top = jnp.max(masked, axis=1)
    for which_bit in range(2):
        partner_top = partner(patch_top, "seq", which_bit)
        patch_top = jnp.maximum(patch_top, partner_top)
    pool_weights = jnp.where(
        member[:, :, None], jnp.exp(masked - patch_top[:, None, :]), 0.0
    ).astype(jnp.bfloat16)
    pool_total = jnp.sum(pool_weights.astype(jnp.float32), axis=1)
    head_values = byte_values.reshape(byte_count, local_heads, -1)
    pool_sum = jnp.einsum(
        "jbg,bgc->jgc", pool_weights, head_values, preferred_element_type=jnp.float32
    )
    for which_bit in range(2):
        partner_sum, partner_total = (
            partner(pool_sum.astype(jnp.bfloat16), "seq", which_bit).astype(pool_sum.dtype),
            partner(pool_total.astype(jnp.bfloat16), "seq", which_bit).astype(pool_total.dtype),
        )
        pool_sum = pool_sum + partner_sum
        pool_total = pool_total + partner_total
    mine_sum = lax.dynamic_slice_in_dim(pool_sum, block_position * patch_count, patch_count, 0)
    mine_total = lax.dynamic_slice_in_dim(pool_total, block_position * patch_count, patch_count, 0)
    pooled = (mine_sum / mine_total[:, :, None]).astype(jnp.bfloat16)
    query_width = GQ * DH
    patch_queries = pooled[:, :, :query_width].reshape(patch_count, local_heads, GQ, DH)
    patch_keys = pooled[:, :, query_width : query_width + DH]
    patch_values = pooled[:, :, query_width + DH :]
    all_keys, all_values = (
        lax.all_gather(patch_keys, "seq", axis=0, tiled=True),
        lax.all_gather(patch_values, "seq", axis=0, tiled=True),
    )
    key_positions = jnp.arange(all_keys.shape[0], dtype=jnp.int32)
    query_positions = device_index * patch_count + jnp.arange(patch_count, dtype=jnp.int32)
    causal = key_positions[None, :] <= query_positions[:, None]
    outputs = []
    for head_group in range(local_heads):
        logits = jnp.einsum(
            "phd,kd->phk",
            patch_queries[:, head_group],
            all_keys[:, head_group],
            preferred_element_type=jnp.float32,
        ) / math.sqrt(DH)
        logits = jnp.where(causal[:, None, :], logits, -1e30)
        highest = jnp.max(logits, axis=-1, keepdims=True)
        raised = jnp.exp(logits - highest)
        attention = (raised / jnp.sum(raised, axis=-1, keepdims=True)).astype(jnp.bfloat16)
        mixed_rows = jnp.einsum(
            "phk,kd->phd", attention, all_values[:, head_group], preferred_element_type=jnp.float32
        )
        outputs.append(mixed_rows.astype(jnp.bfloat16).reshape(patch_count, GQ * DH))
    return jnp.concatenate(outputs, axis=1)


def solution(mesh):
    return jax.shard_map(
        on_device,
        mesh=mesh,
        in_specs=(
            P(("dp", "seq"), None),
            P(),
            P("seq", "mp"),
            P("seq", "mp"),
            P("mp", None),
            P(("dp", "seq")),
        ),
        out_specs=P(("dp", "seq"), "mp"),
        check_vma=False,
    )
```

profile of v0, /device:TPU:1, one launch (start us, length us, event | category | flops | bytes accessed | tf_op | source)
XLA Modules:
  0.0 301.4 jit_solution(7614250328527633074)
XLA Ops:
  6.5 0.0 copy-start
  6.5 0.0 copy-start.1
  6.5 0.0 copy-start.5
  6.5 0.0 all-gather.10.cloned.1.call-start
  6.5 0.7 all-gather.10.cloned.1.call-update
  7.3 0.0 all-gather.6.cloned.1.call-start
  7.3 8.8 %collective-permute-start = (s32[32]{0:T(128)}, s32[32]{0:T(128)S(1)}, u32[]{:S(2)}, u32[]{:S(2)}) collective-permute-start(s32[32]{0:T(128)} %param.11), channel_id=1, source_target_pairs={{0,4},{4,0},{8,12},{12,8},{16,20},{20,16},{24,28},{28,24},{32,36},... | collective-permute-start | bytes 392 | tf_op jit(solution)/shard_map/ppermute | solution.py:19
  16.1 52.4 %all-gather.1 = bf16[128,10,256]{2,1,0:T(8,128)(2,1)S(1)} all-gather(bf16[1,10,256]{2,1,0:T(8,128)(2,1)} %bitcast.84), channel_id=1, replica_groups=mesh['seq'=128,'mp'=2,'dp'=2] {'seq'}, dimensions={0}, use_global_device_ids=true | all-gather | bytes 660480 | tf_op jit(solution)/shard_map/all_gather | solution.py:45
  68.5 0.0 copy-start.2
  68.5 0.2 reshape.131
  68.8 0.0 copy-done.1
  68.8 0.2 fusion.8
  69.0 0.0 copy-done.5
  69.0 0.5 fusion.20
  69.5 0.0 copy-done
  69.5 0.3 fusion.45
  69.8 0.0 collective-permute-done
  69.8 0.0 copy-done.2
  69.8 0.1 broadcast_select_fusion
  69.9 2.4 collective-permute-start.1
  72.3 2.2 collective-permute-done.1
  74.6 0.1 broadcast_select_fusion.1
  74.6 0.1 convert_reduce_fusion.1
  74.8 0.1 select_reduce_fusion
  74.9 2.8 collective-permute-start.2
  77.7 0.8 collective-permute-done.2
  78.5 2.4 collective-permute-start.3
  80.9 2.3 collective-permute-done.3
  83.2 19.7 %all-gather.10.cloned.1.call-done = bf16[128,10,1536]{2,1,0:T(8,128)(2,1)} async-done(((bf16[1,10,1536]{2,1,0:T(8,128)(2,1)}), bf16[128,10,1536]{2,1,0:T(8,128)(2,1)}) %all-gather.10.cloned.1.call-update) | async-done | bytes 3932176 | tf_op jit(solution)/shard_map/all_gather | solution.py:46
  102.9 7.5 %reshape.129 = bf16[1280,1536]{1,0:T(8,128)(2,1)} reshape(bf16[128,10,1536]{2,1,0:T(8,128)(2,1)} %all-gather.10.cloned.1.call-done) | data formatting | bytes 7864320
  110.4 3.3 %convolution_convert_fusion = bf16[256,1536]{1,0:T(8,128)(2,1)S(1)} fusion(bf16[1280,1536]{1,0:T(8,128)(2,1)} %reshape.129, bf16[256,1280]{1,0:T(8,128)(2,1)S(1)} %copy-done.1, f32[1280]{0:T(1024)S(1)} %copy-done.5, f32[256]{0:T(256)S(1)} %add_rsqrt_fusion), kind=kOutput, calls=%fused_computation.10 | convolution fusion | flops 1008336896 | bytes 5380096 | tf_op jit(solution)/shard_map/dot_general | solution.py:49
  113.8 0.3 fusion.42
  114.1 2.2 collective-permute-start.4
  116.3 0.2 convert_reduce_fusion
  116.5 2.2 collective-permute-start.6
  118.7 0.0 collective-permute-done.4
  118.7 0.1 fusion.39
  118.8 2.8 collective-permute-start.5
  121.6 0.0 collective-permute-done.6
  121.6 2.5 collective-permute-start.7
  124.1 7.0 %collective-permute-done.7 = bf16[128,2]{0,1:T(2,128)(2,1)S(1)} collective-permute-done((bf16[128,2]{0,1:T(2,128)(2,1)S(1)}, bf16[128,2]{0,1:T(2,128)(2,1)S(1)}, u32[]{:S(2)}, u32[]{:S(2)}) %collective-permute-start.7) | collective-permute-done | bytes 544 | tf_op jit(solution)/shard_map/ppermute | solution.py:19
  131.1 0.1 constant_dynamic-slice_fusion
  131.2 0.0 collective-permute-done.5
  131.2 0.1 fusion.19
  131.3 0.6 fusion.40
  131.9 0.0 all-gather.6.cloned.1.call-update
  131.9 0.0 all-gather.8.cloned.1.call-start
  132.0 0.7 all-gather.8.cloned.1.call-update
  132.7 0.1 iota_compare_fusion
  132.9 77.9 %all-gather.6.cloned.1.call-done = bf16[4096,2,128]{2,0,1:T(8,128)(2,1)} async-done(((bf16[32,2,128]{2,0,1:T(8,128)(2,1)}), bf16[4096,2,128]{2,0,1:T(8,128)(2,1)}) %all-gather.6.cloned.1.call-update) | async-done | bytes 2097168 | tf_op jit(solution)/shard_map/all_gather | solution.py:84
  210.8 0.0 copy-start.4
  210.8 3.6 %fusion.43 = (f32[32,4]{0,1:T(4,128)S(1)}, f32[32,4,4096]{2,0,1:T(8,128)}) fusion(bf16[4096,2,128]{2,0,1:T(8,128)(2,1)} %all-gather.6.cloned.1.call-done, pred[32,4096]{1,0:T(8,128)(4,1)S(1)} %iota_compare_fusion, bf16[32,1,4,128]{3,2,0,1:T(4,128)(2,1)S(1)} %get-tuple-element.10), kind=kOutput, calls=%fused_computation.77 | convolution fusion | flops 136318976 | bytes 3310080 | tf_op jit(solution)/shard_map/sub | solution.py:100
  214.3 0.0 copy-done.4
  214.3 2.2 fusion.44
  216.5 74.1 %all-gather.8.cloned.1.call-done = bf16[4096,2,128]{2,0,1:T(8,128)(2,1)} async-done(((bf16[32,2,128]{2,0,1:T(8,128)(2,1)}), bf16[4096,2,128]{2,0,1:T(8,128)(2,1)}) %all-gather.8.cloned.1.call-update) | async-done | bytes 2097168 | tf_op jit(solution)/shard_map/all_gather | solution.py:85
  290.6 0.0 copy-start.3
  290.6 0.0 copy-start.6
  290.6 2.5 fusion.12
  293.1 0.0 copy-done.3
  293.1 0.6 copy-done.6
  293.8 0.5 fusion.11
  294.3 0.6 pad_maximum_fusion
  (15 shorter events, 0.1 us)
Async XLA Ops:
  6.5 63.0 %copy-start = (f32[2,128]{1,0:T(2,128)S(1)}, f32[2,128]{1,0:T(2,128)}, u32[]{:S(2)}) copy-start(f32[2,128]{1,0:T(2,128)} %param.10) | copy-start | bytes 3076
  6.5 62.2 %copy-start.1 = (bf16[256,1280]{1,0:T(8,128)(2,1)S(1)}, bf16[256,1280]{1,0:T(8,128)(2,1)}, u32[]{:S(2)}) copy-start(bf16[256,1280]{1,0:T(8,128)(2,1)} %param.6) | copy-start | bytes 1966084
  6.5 62.5 %copy-start.5 = (f32[1280]{0:T(1024)S(1)}, f32[1280]{0:T(1024)}, u32[]{:S(2)}) copy-start(f32[1280]{0:T(1024)} %param.7) | copy-start | bytes 15364
  6.5 96.4 %all-gather.10.cloned.1.call-start = ((), (), s32[]{:S(2)}) async-start(), calls=%async_computation.2 | async-start | bytes 6340608 | tf_op jit(solution)/shard_map/all_gather | solution.py:46
  7.3 203.5 %all-gather.6.cloned.1.call-start = ((), (), s32[]{:S(2)}) async-start(), calls=%async_computation | async-start | bytes 2113536 | tf_op jit(solution)/shard_map/all_gather | solution.py:84
  7.3 62.5 %collective-permute-start = (s32[32]{0:T(128)}, s32[32]{0:T(128)S(1)}, u32[]{:S(2)}, u32[]{:S(2)}) collective-permute-start(s32[32]{0:T(128)} %param.11), channel_id=1, source_target_pairs={{0,4},{4,0},{8,12},{12,8},{16,20},{20,16},{24,28},{28,24},{32,36},... | collective-permute-start | bytes 392 | tf_op jit(solution)/shard_map/ppermute | solution.py:19
  68.5 1.3 copy-start.2
  69.9 4.7 %collective-permute-start.1 = (s32[64]{0:T(128)S(1)}, s32[64]{0:T(128)S(1)}, u32[]{:S(2)}, u32[]{:S(2)}) collective-permute-start(s32[64]{0:T(128)S(1)} %broadcast_select_fusion), channel_id=1, source_target_pairs={{0,8},{8,0},{4,12},{12,4},{16,24},{24,16},{20,28},{28,20},{32,40},... | collective-permute-start | bytes 776 | tf_op jit(solution)/shard_map/ppermute | solution.py:19
  74.9 3.6 %collective-permute-start.2 = (f32[128,2]{0,1:T(2,128)S(1)}, f32[128,2]{0,1:T(2,128)S(1)}, u32[]{:S(2)}, u32[]{:S(2)}) collective-permute-start(f32[128,2]{0,1:T(2,128)S(1)} %select_reduce_fusion), channel_id=1, source_target_pairs={{0,4},{4,0},{8,12},{12,8},{16,20},{20,16},{24,28},{28,24},{32,36},... | collective-permute-start | bytes 3080 | tf_op jit(solution)/shard_map/ppermute | solution.py:19
  78.5 4.7 %collective-permute-start.3 = (f32[128,2]{0,1:T(2,128)S(1)}, f32[128,2]{0,1:T(2,128)S(1)}, u32[]{:S(2)}, u32[]{:S(2)}) collective-permute-start(f32[128,2]{0,1:T(2,128)S(1)} %max.6), channel_id=1, source_target_pairs={{0,8},{8,0},{4,12},{12,4},{16,24},{24,16},{20,28},{28,20},{32,40},... | collective-permute-start | bytes 3080 | tf_op jit(solution)/shard_map/ppermute | solution.py:19
  114.1 4.6 %collective-permute-start.4 = (bf16[128,2,768]{2,0,1:T(8,128)(2,1)S(1)}, bf16[128,2,768]{2,0,1:T(8,128)(2,1)S(1)}, u32[]{:S(2)}, u32[]{:S(2)}) collective-permute-start(bf16[128,2,768]{2,0,1:T(8,128)(2,1)S(1)} %get-tuple-element.11), channel_id=1, source_target_pairs={{0,4},{4,0},{8,12},{12,8},{16,20},{20,16},{24,28},{28,24},{32,36},... | collective-permute-start | bytes 1179656 | tf_op jit(solution)/shard_map/ppermute | solution.py:19
  116.5 5.1 %collective-permute-start.6 = (bf16[128,2]{0,1:T(2,128)(2,1)S(1)}, bf16[128,2]{0,1:T(2,128)(2,1)S(1)}, u32[]{:S(2)}, u32[]{:S(2)}) collective-permute-start(bf16[128,2]{0,1:T(2,128)(2,1)S(1)} %convert_element_type.67), channel_id=1, source_target_pairs={{0,4},{4,0},{8,12},{12,8},{16,20},{20,16},{24,28},{28,24},{32,36},... | collective-permute-start | bytes 1544 | tf_op jit(solution)/shard_map/ppermute | solution.py:19
  118.8 12.4 %collective-permute-start.5 = (bf16[128,2,768]{2,0,1:T(8,128)(2,1)S(1)}, bf16[128,2,768]{2,0,1:T(8,128)(2,1)S(1)}, u32[]{:S(2)}, u32[]{:S(2)}) collective-permute-start(bf16[128,2,768]{2,0,1:T(8,128)(2,1)S(1)} %get-tuple-element.5), channel_id=1, source_target_pairs={{0,8},{8,0},{4,12},{12,4},{16,24},{24,16},{20,28},{28,20},{32,40},... | collective-permute-start | bytes 1179656 | tf_op jit(solution)/shard_map/ppermute | solution.py:19
  121.6 9.5 %collective-permute-start.7 = (bf16[128,2]{0,1:T(2,128)(2,1)S(1)}, bf16[128,2]{0,1:T(2,128)(2,1)S(1)}, u32[]{:S(2)}, u32[]{:S(2)}) collective-permute-start(bf16[128,2]{0,1:T(2,128)(2,1)S(1)} %fusion.32), channel_id=1, source_target_pairs={{0,8},{8,0},{4,12},{12,4},{16,24},{24,16},{20,28},{28,20},{32,40},... | collective-permute-start | bytes 1544 | tf_op jit(solution)/shard_map/ppermute | solution.py:19
  131.9 158.7 %all-gather.8.cloned.1.call-start = ((), (), s32[]{:S(2)}) async-start(), calls=%async_computation.1 | async-start | bytes 2113536 | tf_op jit(solution)/shard_map/all_gather | solution.py:85
  210.8 3.6 %copy-start.4 = (bf16[4096,2,128]{2,0,1:T(8,128)(2,1)S(1)}, bf16[4096,2,128]{2,0,1:T(8,128)(2,1)}, u32[]{:S(2)}) copy-start(bf16[4096,2,128]{2,0,1:T(8,128)(2,1)} %all-gather.6.cloned.1.call-done) | copy-start | bytes 6291460
  290.6 2.5 copy-start.3
  290.6 3.2 %copy-start.6 = (f32[32,4,4096]{2,0,1:T(8,128)S(1)}, f32[32,4,4096]{2,0,1:T(8,128)}, u32[]{:S(2)}) copy-start(f32[32,4,4096]{2,0,1:T(8,128)} %get-tuple-element.16) | copy-start | bytes 6291460
Sparse Core Ops, SparseCore 0:
  10.5 92.3 all-gather.9
  132.1 78.6 all-gather.5
  213.8 76.7 all-gather.7
where the time goes:
time: 302 us; the launch traced here: 301 us
  waiting for transfers between devices  185 us (61%)
  blocking collectives  52.4 us (17%)
  starting transfers between devices  26.1 us (9%)
  between operations  13.5 us (4%)
  matrix products  13.1 us (4%)
  local copies, waits for them, and re-layouts  9.19 us (3%)
    all_gather x1, waiting for transfers between devices, on_device(): lax.all_gather(patch_keys, 'seq', axis=0, tiled=True)  77.9 us
    all_gather x1, waiting for transfers between devices, on_device(): lax.all_gather(patch_values, 'seq', axis=0, tiled=True)  74.1 us
    all_gather x1, blocking collectives, on_device(): lax.all_gather(key_weight, 'seq', axis=0, tiled=True)  52.4 us
    ppermute x8, starting transfers between devices, partner(): return lax.ppermute(block, axis, route)  26 us
    all_gather x1, waiting for transfers between devices, on_device(): lax.all_gather(value_weight, 'seq', axis=0, tiled=True)  19.7 us
    ppermute x8, waiting for transfers between devices, partner(): return lax.ppermute(block, axis, route)  12.4 us
    unnamed x16, local copies, waits for them, and re-layouts  8.44 us
  transfers between devices with their start and end apart: 11, of which 7 were waited for; matrix products, arithmetic and copies ran while one was open for 3% of the time, Pallas kernels for 0%

commit v1 on v0

v1 whole, which is shorter than its diff:
```python
import functools
import math

import jax
import jax.numpy as jnp
from jax import lax
from jax.experimental import pallas as pl
from jax.experimental.pallas import tpu as pltpu
from jax.sharding import PartitionSpec as P

DH = 128
GQ = 4
VW = 768
HALF = 32
LANES = 256
NEG = -1e30
MESH = pl.DeviceIdType.MESH
f32 = jnp.float32
bf16 = jnp.bfloat16


def iota(shape, dim):
    return lax.broadcasted_iota(jnp.int32, shape, dim)


def dot(a, b, dims=((1,), (0,))):
    return lax.dot_general(a, b, (dims, ((), ())), preferred_element_type=f32)


def kernel(
    side,
    bytes_ref,
    gain_ref,
    kw_ref,
    vw_ref,
    pq_ref,
    starts_ref,
    out_ref,
    wbuf,
    kvbuf,
    wstage,
    sib_bytes,
    normed,
    starts_buf,
    key_stage,
    key_recv,
    key_z,
    key_y,
    send_rows,
    own_rows,
    got_rows,
    send_stats,
    got_stats,
    spread,
    top_ref,
    total_ref,
    mix_ref,
    out_send,
    out_got,
    w_recv,
    kv_recv,
    sib_recv,
    starts_recv,
    keyz_recv,
    keyy_recv,
    pair_recv,
    out_recv,
    w_send,
    kv_send,
    sib_send,
    starts_send,
    keyz_send,
    keyy_send,
    pair_send,
    out_send_sem,
):
    me = lax.axis_index("seq")
    core = lax.rem(me, 2)
    y = lax.rem(me // 2, side)
    z = me // (2 * side)
    chip = me // 2
    block_at = lax.rem(me, 4)
    pair_at = lax.rem(chip, 2)
    width = bytes_ref.shape[1]
    rows = bytes_ref.shape[0]

    def at(zz, yy, cc):
        return (zz * side + yy) * 2 + cc

    sibling = at(z, y, 1 - core)
    pair_y = y + 1 - 2 * pair_at
    pair = at(z, pair_y, core)
    cross = at(z, pair_y, 1 - core)

    def wrap(index):
        return lax.rem(index + 2 * side, side)

    def copy(src, dst, send_sem, recv_sem, target):
        return pltpu.make_async_remote_copy(
            src_ref=src,
            dst_ref=dst,
            send_sem=send_sem,
            recv_sem=recv_sem,
            device_id={"seq": target},
            device_id_type=MESH,
        )

    def arrived(ref, sem):
        pltpu.make_async_copy(ref, ref, sem).wait()

    barrier = pltpu.get_barrier_semaphore()

    def greet(target):
        pl.semaphore_signal(barrier, inc=1, device_id={"seq": target}, device_id_type=MESH)

    @pl.loop(1, side)
    def _(i):
        greet(at(wrap(z + i), y, core))
        greet(at(z, wrap(y + i), core))

    greet(sibling)
    greet(cross)

    part = vw_ref[...].astype(f32)
    depth = part.shape[0]
    pieces = []
    for head in range(2):
        cuts = [part[:, head * VW + n * LANES : head * VW + (n + 1) * LANES] for n in range(VW // LANES)]
        cuts.append(jnp.zeros((HALF - depth * len(cuts), LANES), f32))
        pieces.append(jnp.concatenate(cuts, axis=0).astype(bf16))
    first_core = core == 0
    wbuf[z, y, core] = jnp.where(first_core, pieces[0], pieces[1])
    wstage[...] = jnp.where(first_core, pieces[1], pieces[0])

    folded = kw_ref[...].astype(f32)
    row_at = iota((depth, 128), 0)
    lane_at = iota((depth, 128), 1)
    keyed = []
    for head in range(2):
        col = jnp.sum(folded[:, head * DH : (head + 1) * DH] * pq_ref[head : head + 1, :], axis=1, keepdims=True)
        keyed.append(jnp.sum(jnp.where(lane_at == row_at + core * 16, col, 0.0), axis=0, keepdims=True))
    key_stage[0] = jnp.where(first_core, keyed[1], keyed[0])
    key_own = jnp.where(first_core, keyed[0], keyed[1])

    starts_buf[block_at] = jnp.concatenate(
        [starts_ref[...], jnp.zeros((1, 128 - starts_ref.shape[1]), jnp.int32)], axis=1
    )

    pl.semaphore_wait(barrier, 2 * side)

    to_sibling = [
        copy(key_stage, key_recv, sib_send.at[0], sib_recv.at[0], sibling),
        copy(wstage, wbuf.at[z, y, core], sib_send.at[1], sib_recv.at[1], sibling),
        copy(bytes_ref, sib_bytes, sib_send.at[2], sib_recv.at[2], sibling),
    ]
    for one in to_sibling:
        one.start()
    to_block = [
        copy(starts_buf.at[block_at], starts_buf.at[block_at], starts_send.at[k], starts_recv.at[block_at], target)
        for k, target in enumerate((sibling, pair, cross))
    ]
    for one in to_block:
        one.start()

    def ref_of(buf, half, a, b):
        return buf.at[a, b, 0] if half == 0 else buf.at[b, a, 1]

    def dev_of(half, a, b):
        return at(a, b, core) if half == 0 else at(b, a, core)

    def own_of(half):
        return (z, y) if half == 0 else (y, z)

    def sem_of(sems, half, a, b):
        return sems.at[a, b, 0] if half == 0 else sems.at[b, a, 1]

    def ring(buf, recv, send, half, a, b, step):
        a0, b0 = own_of(half)
        ref = ref_of(buf, half, a, b)
        copy(
            ref, ref, send.at[half, 1], sem_of(recv, half, a, b), dev_of(half, a0, wrap(b0 + step))
        ).start()

    def pass_on(buf, recv, send, half, a, b, step, distance, even):
        last = distance == side // 2 - 1
        if not last or even == (step == 1):
            ring(buf, recv, send, half, a, b, step)

    def begin(buf, recv, send, half):
        a0, b0 = own_of(half)
        ref = ref_of(buf, half, a0, b0)
        for step in (1, -1):
            pass_on(buf, recv, send, half, a0, b0, step, 0, True)

        @pl.loop(1, side)
        def _(i):
            copy(
                ref, ref, send.at[half, 0], sem_of(recv, half, a0, b0), dev_of(half, wrap(a0 + i), b0)
            ).start()

    def visit(buf, recv, send, distance, t):
        for half in (0, 1):
            a0, b0 = own_of(half)
            for even, a in ((True, wrap(a0 - t)), (False, wrap(a0 + t + 1))):
                if distance == 0:

                    def take(half=half, a=a, b0=b0, even=even):
                        arrived(ref_of(buf, half, a, b0), sem_of(recv, half, a, b0))
                        for step in (1, -1):
                            pass_on(buf, recv, send, half, a, b0, step, 0, even)

                    if even:
                        pl.when(t > 0)(take)
                    else:
                        take()
                elif distance < side // 2:
                    for step in (1, -1):
                        b = wrap(b0 - step * distance)
                        arrived(ref_of(buf, half, a, b), sem_of(recv, half, a, b))
                        pass_on(buf, recv, send, half, a, b, step, distance, even)
                else:
                    b = wrap(b0 + distance)
                    arrived(ref_of(buf, half, a, b), sem_of(recv, half, a, b))

    def stage(buf, recv, send, distance):
        @pl.loop(0, side // 2)
        def _(t):
            visit(buf, recv, send, distance, t)

    def sent(buf, send):
        for half in (0, 1):
            ref = buf.at[0, pl.ds(0, side - 1), half]
            arrived(ref, send.at[half, 0])
            ref = buf.at[:, pl.ds(0, side - 1), half]
            arrived(ref, send.at[half, 1])

    weights = (wbuf, w_recv, w_send)
    sib_piece = wbuf.at[z, y, 1 - core]

    @pl.when(first_core)
    def _():
        begin(*weights, 0)
        arrived(sib_piece, sib_recv.at[1])
        begin(*weights, 1)

    @pl.when(core == 1)
    def _():
        begin(*weights, 1)
        arrived(sib_piece, sib_recv.at[1])
        begin(*weights, 0)

    arrived(key_recv, sib_recv.at[0])
    key_z[z] = key_own + key_recv[0]

    @pl.loop(1, side)
    def _(i):
        copy(key_z.at[z], key_z.at[z], keyz_send, keyz_recv.at[z], at(wrap(z + i), y, core)).start()

    def norm_rows(ref, first):
        @pl.loop(0, rows // 32)
        def _(i):
            at_row = pl.multiple_of(i * 32, 32)
            wide = ref[pl.ds(at_row, 32), :].astype(f32)
            scale = lax.rsqrt(jnp.mean(wide * wide, axis=-1, keepdims=True) + 1e-05)
            normed[pl.ds(pl.multiple_of(first + at_row, 32), 32), :] = (wide * scale * gain_ref[...]).astype(bf16)

    norm_rows(bytes_ref, core * rows)

    @pl.loop(1, side)
    def _(i):
        other = wrap(z + i)
        arrived(key_z.at[other], keyz_recv.at[other])

    key_y[y] = jnp.concatenate([key_z[i] for i in range(side)], axis=0)

    @pl.loop(1, side)
    def _(i):
        copy(key_y.at[y], key_y.at[y], keyy_send, keyy_recv.at[y], at(z, wrap(y + i), core)).start()

    stage(*weights, 0)
    arrived(sib_bytes, sib_recv.at[2])
    norm_rows(sib_bytes, (1 - core) * rows)
    if side > 2:
        stage(*weights, 1)

    @pl.loop(1, side)
    def _(i):
        other = wrap(y + i)
        arrived(key_y.at[other], keyy_recv.at[other])

    chips = side * side
    table = key_y[...].reshape(chips, 128)
    high = table.astype(bf16).astype(f32)
    middle = (table - high).astype(bf16).astype(f32)
    low = (table - high - middle).astype(bf16).astype(f32)
    packed = (high + pltpu.roll(middle, 32, axis=1) + pltpu.roll(low, 64, axis=1)).astype(bf16)
    column = iota((1, width), 1)
    column_chip = column // (2 * depth)
    column_row = lax.rem(column_chip, side) * side + column_chip // side
    pick = jnp.where(iota((chips, width), 0) == column_row, 1.0, 0.0).astype(bf16)
    taken = dot(packed, pick, ((0,), (0,)))
    column_lane = lax.rem(column // depth, 2) * 16 + lax.rem(column, depth)
    lane_row = iota((128, width), 0)
    key_rows = jnp.where(lax.rem(lane_row, 32) == column_lane, taken, 0.0).astype(bf16)
    scores = jnp.sum(dot(key_rows, normed[...], ((1,), (1,))), axis=0, keepdims=True) / math.sqrt(DH)

    for k in range(1, 4):
        other = lax.rem(block_at + k, 4)
        arrived(starts_buf.at[other], starts_recv.at[other])
    patch_sub = iota((HALF, 128), 0)
    patch_lane = iota((HALF, 128), 1)
    first_cols, next_cols = [], []
    for q in range(4):
        row = starts_buf[q]
        follow = (chip // 2 + 1) * (4 * rows) if q == 3 else starts_buf[q + 1][:, 0:1]
        row = jnp.where(iota((1, 128), 1) == HALF, follow, row)
        first_cols.append(jnp.sum(jnp.where(patch_lane == patch_sub, row, 0), axis=1, keepdims=True))
        next_cols.append(jnp.sum(jnp.where(patch_lane == patch_sub + 1, row, 0), axis=1, keepdims=True))
    first_col = jnp.concatenate(first_cols, axis=0)
    next_col = jnp.concatenate(next_cols, axis=0)
    position = chip * (2 * rows) + iota((1, 2 * rows), 1)
    member = (first_col <= position) & (position < next_col)

    masked = jnp.where(member, scores, NEG)
    top = jnp.max(masked, axis=1, keepdims=True)
    weight = jnp.where(member, jnp.exp(masked - top), 0.0).astype(bf16)
    total = jnp.sum(weight.astype(f32), axis=1, keepdims=True)
    share = jnp.where(total > 0.0, 1.0 / jnp.maximum(total, 1e-30), 0.0)
    pooled_rows = dot(weight, normed[...]) * share
    half_rows = 2 * HALF
    own_rows[...] = pooled_rows.reshape(2, half_rows, width)
    send_rows[...] = pooled_rows.astype(bf16).reshape(2, half_rows, width)
    eye = iota((4 * HALF, 128), 0) == iota((4 * HALF, 128), 1)
    top_row = jnp.sum(jnp.where(eye, top, 0.0), axis=0, keepdims=True)
    total_row = jnp.sum(jnp.where(eye, total, 0.0), axis=0, keepdims=True)
    stats = jnp.concatenate([top_row, total_row, jnp.zeros((6, 128), f32)], axis=0)
    send_stats[...] = stats
    to_pair = [
        copy(send_rows.at[1 - pair_at], got_rows, pair_send.at[0], pair_recv.at[0], pair),
        copy(send_stats, got_stats, pair_send.at[1], pair_recv.at[1], pair),
    ]
    for one in to_pair:
        one.start()

    for distance in range(2, side // 2):
        stage(*weights, distance)

    for one in to_pair:
        one.wait_recv()
    eye = iota((half_rows, 128), 1) == iota((half_rows, 128), 0) + pair_at * half_rows

    def to_column(row):
        return jnp.sum(jnp.where(eye, row, 0.0), axis=1, keepdims=True)

    own_top, own_total = to_column(send_stats[0:1, :]), to_column(send_stats[1:2, :])
    got_top, got_total = to_column(got_stats[0:1, :]), to_column(got_stats[1:2, :])
    top = jnp.maximum(own_top, got_top)
    own_part = jnp.exp(own_top - top) * own_total
    got_part = jnp.exp(got_top - top) * got_total
    share = 1.0 / (own_part + got_part)
    merged = own_rows[pair_at] * (own_part * share) + got_rows[...].astype(f32) * (got_part * share)
    merged = merged.astype(bf16)

    lane = iota((1, 128), 1)
    in_piece = lax.rem(lane, HALF)
    which = in_piece // depth
    source = jnp.where(in_piece < 3 * depth, (lane // HALF) * depth + lax.rem(in_piece, depth), -100000)
    window = min(256, width)
    sub = iota((window, 128), 0)
    for b in range(wbuf.shape[0] * side * 2 * HALF // 128):
        left = min(4 * depth * b // 128 * 128, width - window)
        choose = jnp.where(sub == source + (4 * depth * b - left), 1.0, 0.0).astype(bf16)
        block = dot(merged[:, left : left + window], choose)
        for n in range(3):
            spread[n * half_rows : (n + 1) * half_rows, b * 128 : (b + 1) * 128] = jnp.where(
                which == n, block, 0.0
            ).astype(bf16)

    stage(*weights, side // 2)
    mapped = jnp.zeros((3 * half_rows, LANES), f32)
    span = side * 2 * HALF
    for zz in range(side):
        mapped = mapped + dot(spread[:, zz * span : (zz + 1) * span], wbuf[zz].reshape(span, LANES))
    mapped = mapped.astype(bf16)
    kvbuf[z, y] = mapped[2 * half_rows :].reshape(2, HALF, LANES)
    queries = jnp.concatenate(
        [mapped[n * half_rows : (n + 1) * half_rows, k * DH : (k + 1) * DH] for n in range(2) for k in range(2)],
        axis=0,
    )

    patches = (kvbuf, kv_recv, kv_send)
    begin(*patches, 0)
    begin(*patches, 1)

    query_at = chip * half_rows + lax.rem(iota((1, GQ * half_rows), 1), half_rows)
    key_index = iota((side * HALF, 1), 0)
    top_ref[...] = jnp.full(top_ref.shape, NEG, f32)
    total_ref[...] = jnp.zeros(total_ref.shape, f32)
    mix_ref[...] = jnp.zeros(mix_ref.shape, f32)

    def attend(half, b):
        if half == 0:
            pair_of = kvbuf[:, b, 0]
            key_at = (key_index // HALF * side + b) * half_rows
        else:
            pair_of = kvbuf[b, :, 1]
            key_at = (key_index // HALF + b * side) * half_rows + HALF
        pair_of = pair_of.reshape(side * HALF, LANES)
        logits = dot(pair_of[:, :DH], queries, ((1,), (1,))) / math.sqrt(DH)
        logits = jnp.where(key_at + lax.rem(key_index, HALF) <= query_at, logits, NEG)
        old = top_ref[...]
        new = jnp.maximum(old, jnp.max(logits, axis=0, keepdims=True))
        raised = jnp.exp(logits - new)
        keep = jnp.exp(old - new)
        top_ref[...] = new
        total_ref[...] = total_ref[...] * keep + jnp.sum(raised, axis=0, keepdims=True)
        mix_ref[...] = mix_ref[...] * keep + dot(pair_of[:, DH:], raised.astype(bf16), ((0,), (0,)))

    stage(*patches, 0)
    for distance in range(1, side // 2 + 1):
        stage(*patches, distance)
        for half in (0, 1):
            b0 = own_of(half)[1]
            if distance == 1:
                attend(half, b0)
            else:
                attend(half, wrap(b0 + distance - 1))
                attend(half, wrap(b0 - distance + 1))
    for half in (0, 1):
        attend(half, wrap(own_of(half)[1] + side // 2))

    mixed = (mix_ref[...] / total_ref[...]).T
    mixed = jnp.concatenate([mixed[h * half_rows : (h + 1) * half_rows] for h in range(GQ)], axis=1).astype(bf16)
    own_out = jnp.where(first_core, mixed[:HALF], mixed[HALF:])
    out_send[...] = jnp.where(first_core, mixed[HALF:], mixed[:HALF])
    last = copy(out_send, out_got, out_send_sem, out_recv, sibling)
    last.start()
    for one in to_sibling[:1] + to_sibling[2:] + to_block + to_pair:
        one.wait_send()
    to_sibling[1].wait_send()
    arrived(key_z.at[pl.ds(0, side - 1)], keyz_send)
    arrived(key_y.at[pl.ds(0, side - 1)], keyy_send)
    sent(wbuf, w_send)
    sent(kvbuf, kv_send)
    last.wait()
    theirs = out_got[...]
    out_ref[:, : GQ * DH] = jnp.where(first_core, own_out, theirs)
    out_ref[:, GQ * DH :] = jnp.where(first_core, theirs, own_out)


def on_device(seq, byte_rows, norm_gain, key_weight, value_weight, pool_query, patch_starts):
    side = math.isqrt(seq // 2)
    rows, width = byte_rows.shape
    gathered = (side, side, 2, HALF, LANES)
    dma = pltpu.SemaphoreType.DMA
    scratch = [
        pltpu.VMEM(gathered, bf16),
        pltpu.VMEM(gathered, bf16),
        pltpu.VMEM((HALF, LANES), bf16),
        pltpu.VMEM((rows, width), bf16),
        pltpu.VMEM((2 * rows, width), bf16),
        pltpu.VMEM((4, 1, 128), jnp.int32),
        pltpu.VMEM((1, 1, 128), f32),
        pltpu.VMEM((1, 1, 128), f32),
        pltpu.VMEM((side, 1, 128), f32),
        pltpu.VMEM((side, side, 128), f32),
        pltpu.VMEM((2, 2 * HALF, width), bf16),
        pltpu.VMEM((2, 2 * HALF, width), f32),
        pltpu.VMEM((2 * HALF, width), bf16),
        pltpu.VMEM((8, 128), f32),
        pltpu.VMEM((8, 128), f32),
        pltpu.VMEM((6 * HALF, side * side * 2 * HALF), bf16),
        pltpu.VMEM((1, 2 * HALF * GQ), f32),
        pltpu.VMEM((1, 2 * HALF * GQ), f32),
        pltpu.VMEM((DH, 2 * HALF * GQ), f32),
        pltpu.VMEM((HALF, GQ * DH), bf16),
        pltpu.VMEM((HALF, GQ * DH), bf16),
        dma((side, side, 2)),
        dma((side, side, 2)),
        dma((3,)),
        dma((4,)),
        dma((side,)),
        dma((side,)),
        dma((2,)),
        dma(()),
        dma((2, 2)),
        dma((2, 2)),
        dma((3,)),
        dma((3,)),
        dma(()),
        dma(()),
        dma((2,)),
        dma(()),
    ]
    vmem = pl.BlockSpec(memory_space=pltpu.VMEM)
    return pl.pallas_call(
        functools.partial(kernel, side),
        out_shape=jax.ShapeDtypeStruct((HALF, 2 * GQ * DH), bf16),
        in_specs=[vmem] * 6,
        out_specs=vmem,
        scratch_shapes=scratch,
        compiler_params=pltpu.CompilerParams(
            collective_id=0, has_side_effects=True, vmem_limit_bytes=48 * 1024 * 1024
        ),
    )(
        byte_rows,
        norm_gain.reshape(1, width),
        key_weight,
        value_weight,
        pool_query,
        patch_starts.reshape(1, -1),
    )


def solution(mesh):
    return jax.shard_map(
        functools.partial(on_device, mesh.shape["seq"]),
        mesh=mesh,
        in_specs=(
            P(("dp", "seq"), None),
            P(),
            P("seq", "mp"),
            P("seq", "mp"),
            P("mp", None),
            P(("dp", "seq")),
        ),
        out_specs=P(("dp", "seq"), "mp"),
        check_vma=False,
    )
```

time: 302 us -> 71.3 us (0.24)
  waiting for transfers between devices: 185 us -> 0 us
  Pallas kernels: 0 us -> 67.7 us
  blocking collectives: 52.4 us -> 0 us
  starting transfers between devices: 26.1 us -> 0 us
  between operations: 13.5 us -> 0.03 us
  matrix products: 13.1 us -> 0 us
  local copies, waits for them, and re-layouts: 9.19 us -> 3.26 us
    all_gather x3 -> x0, waiting for transfers between devices: 172 us -> none  [the longest x1 77.9 us: on_device(): lax.all_gather(patch_keys, 'seq', axis=0, tiled=True)]
    pallas_call x0 -> x1, Pallas kernels: none -> 67.7 us  [on_device(): pl.pallas_call(functools.partial(kernel, side), out_shape=jax.ShapeDtypeS...]
    all_gather x1 -> x0, blocking collectives: 52.4 us -> none  [on_device(): lax.all_gather(key_weight, 'seq', axis=0, tiled=True)]
    ppermute x8 -> x0, starting transfers between devices: 26 us -> none  [partner(): return lax.ppermute(block, axis, route)]
    ppermute x8 -> x0, waiting for transfers between devices: 12.4 us -> none  [partner(): return lax.ppermute(block, axis, route)]
    dot_general x6 -> x0, matrix products: 7.36 us -> none  [the longest x1 3.33 us: on_device(): jnp.dot(normed, full_values, preferred_element_type=jnp.float32)]
    unnamed x16 -> x11, local copies, waits for them, and re-layouts: 8.44 us -> 2.52 us
    sub x2 -> x0, matrix products: 5.76 us -> none  [on_device(): raised = jnp.exp(logits - highest)]
  transfers between devices with their start and end apart: 11 -> 0, of which waited for: 7 -> 0; matrix products, arithmetic and copies ran while one was open for 3% -> 0% of each run, Pallas kernels for 0% -> 0%
where the time goes in v1:
time: 71.3 us; the launch traced here: 71 us
  Pallas kernels  67.7 us (95%)
  local copies, waits for them, and re-layouts  3.26 us (5%)
    pallas_call x1, Pallas kernels, on_device(): pl.pallas_call(functools.partial(kernel, side), out_shape=jax.ShapeDtypeS...  67.7 us
    unnamed x11, local copies, waits for them, and re-layouts  2.52 us

profile of v1, /device:TPU:1, one launch (start us, length us, event | category | flops | bytes accessed | tf_op | source)
XLA Modules:
  0.0 71.0 jit_solution(850825875740512811)
XLA Ops:
  0.0 0.0 copy-start.2
  0.0 0.0 copy-start.3
  0.0 0.0 copy-start.4
  0.0 0.7 %reshape.6.gain_ref = f32[1,1280]{1,0:T(1,128)S(1)} reshape(f32[1280]{0:T(1024)} %param.7) | data formatting | bytes 10240 | tf_op jit(solution)/shard_map/reshape | solution.py:507
  0.7 0.0 copy-done.2
  0.8 0.0 copy-done.3
  0.8 0.0 copy-done.4
  0.8 0.0 copy-start
  0.8 1.1 %copy-done = bf16[256,1280]{1,0:T(8,128)(2,1)S(1)} copy-done((bf16[256,1280]{1,0:T(8,128)(2,1)S(1)}, bf16[256,1280]{1,0:T(8,128)(2,1)}, u32[]{:S(2)}) %copy-start) | copy-done | bytes 655384
  1.9 0.0 copy-start.1
  1.9 0.8 %copy-done.1 = bf16[10,1536]{1,0:T(8,128)(2,1)S(1)} copy-done((bf16[10,1536]{1,0:T(8,128)(2,1)S(1)}, bf16[10,1536]{1,0:T(8,128)(2,1)}, u32[]{:S(2)}) %copy-start.1) | copy-done | bytes 30744
  2.7 67.7 %shard_map.64 = bf16[32,1024]{1,0:T(8,128)(2,1)S(1)} custom-call(bf16[256,1280]{1,0:T(8,128)(2,1)S(1)} %copy-done, f32[1,1280]{1,0:T(1,128)S(1)} %reshape.6.gain_ref, bf16[10,256]{1,0:T(8,128)(2,1)S(1)} %copy-done.2, bf16[10,1536]{1,0:T(8,128)(2,1)S(1)} %copy-done.1, f32[2,128]{1,0:T(2,128)S(1)} %copy-done.3, s32[1,32]{1,0:T(1,128)S(1)} %bitcast.1), custom_call_target="tpu_custom_call" | custom-call | tf_op jit(solution)/shard_map/pallas_call | solution.py:496
  70.4 0.6 copy.8
Async XLA Ops:
  0.0 0.8 %copy-start.2 = (bf16[10,256]{1,0:T(8,128)(2,1)S(1)}, bf16[10,256]{1,0:T(8,128)(2,1)}, u32[]{:S(2)}) copy-start(bf16[10,256]{1,0:T(8,128)(2,1)} %kw_ref.1) | copy-start | bytes 15364
  0.0 0.8 %copy-start.3 = (f32[2,128]{1,0:T(2,128)S(1)}, f32[2,128]{1,0:T(2,128)}, u32[]{:S(2)}) copy-start(f32[2,128]{1,0:T(2,128)} %pq_ref.1) | copy-start | bytes 3076
  0.0 0.8 %copy-start.4 = (s32[32]{0:T(128)S(1)}, s32[32]{0:T(128)}, u32[]{:S(2)}) copy-start(s32[32]{0:T(128)} %param.11) | copy-start | bytes 388
  0.8 1.1 %copy-start = (bf16[256,1280]{1,0:T(8,128)(2,1)S(1)}, bf16[256,1280]{1,0:T(8,128)(2,1)}, u32[]{:S(2)}) copy-start(bf16[256,1280]{1,0:T(8,128)(2,1)} %bytes_ref.1) | copy-start | bytes 1966084
  1.9 0.8 %copy-start.1 = (bf16[10,1536]{1,0:T(8,128)(2,1)S(1)}, bf16[10,1536]{1,0:T(8,128)(2,1)}, u32[]{:S(2)}) copy-start(bf16[10,1536]{1,0:T(8,128)(2,1)} %vw_ref.1) | copy-start | bytes 92164

commit v2 on v1

v2 whole, which is shorter than its diff:
```python
import functools
import math

import jax
import jax.numpy as jnp
from jax import lax
from jax.experimental import pallas as pl
from jax.experimental.pallas import tpu as pltpu
from jax.sharding import PartitionSpec as P

DH = 128
GQ = 4
VW = 768
HALF = 32
LANES = 256
NEG = -1e30
MESH = pl.DeviceIdType.MESH
f32 = jnp.float32
bf16 = jnp.bfloat16


def iota(shape, dim):
    return lax.broadcasted_iota(jnp.int32, shape, dim)


def dot(a, b, dims=((1,), (0,))):
    return lax.dot_general(a, b, (dims, ((), ())), preferred_element_type=f32)


def kernel(
    side,
    bytes_in,
    gain_in,
    kw_in,
    vw_in,
    pq_in,
    starts_in,
    out_ref,
    bytes_ref,
    gain_ref,
    kw_ref,
    vw_ref,
    pq_ref,
    starts_ref,
    wbuf,
    kvbuf,
    wstage,
    sib_bytes,
    normed,
    starts_buf,
    key_stage,
    key_z,
    key_y,
    send_rows,
    own_rows,
    got_rows,
    send_stats,
    got_stats,
    spread,
    pick_ref,
    lane_ref,
    member_ref,
    choose_ref,
    top_ref,
    total_ref,
    mix_ref,
    out_send,
    out_got,
    load_sem,
    w_recv,
    kv_recv,
    sib_recv,
    starts_recv,
    keyz_recv,
    keyy_recv,
    pair_recv,
    out_recv,
    w_send,
    kv_send,
    sib_send,
    starts_send,
    keyz_send,
    keyy_send,
    pair_send,
    out_send_sem,
):
    me = lax.axis_index("seq")
    core = lax.rem(me, 2)
    y = lax.rem(me // 2, side)
    z = me // (2 * side)
    chip = me // 2
    block_at = lax.rem(me, 4)
    pair_at = lax.rem(chip, 2)
    width = bytes_ref.shape[1]
    rows = bytes_ref.shape[0]

    def at(zz, yy, cc):
        return (zz * side + yy) * 2 + cc

    sibling = at(z, y, 1 - core)
    pair_y = y + 1 - 2 * pair_at
    pair = at(z, pair_y, core)
    cross = at(z, pair_y, 1 - core)

    def wrap(index):
        return lax.rem(index + 2 * side, side)

    def copy(src, dst, send_sem, recv_sem, target):
        return pltpu.make_async_remote_copy(
            src_ref=src,
            dst_ref=dst,
            send_sem=send_sem,
            recv_sem=recv_sem,
            device_id={"seq": target},
            device_id_type=MESH,
        )

    def arrived(ref, sem):
        pltpu.make_async_copy(ref, ref, sem).wait()

    loads = [
        pltpu.make_async_copy(src, dst, load_sem.at[k])
        for k, (src, dst) in enumerate(
            (
                (kw_in, kw_ref),
                (pq_in, pq_ref),
                (vw_in, vw_ref),
                (starts_in, starts_ref),
                (bytes_in, bytes_ref),
                (gain_in, gain_ref),
            )
        )
    ]
    for one in loads:
        one.start()

    barrier = pltpu.get_barrier_semaphore()

    def greet(target):
        pl.semaphore_signal(barrier, inc=1, device_id={"seq": target}, device_id_type=MESH)

    @pl.loop(1, side)
    def _(i):
        greet(at(wrap(z + i), y, core))
        greet(at(wrap(z + i), y, 1 - core))
        greet(at(z, wrap(y + i), core))

    greet(sibling)
    greet(cross)

    for one in loads[:2]:
        one.wait()
    folded = kw_ref[...].astype(f32)
    depth = folded.shape[0]
    row_at = iota((depth, 128), 0)
    lane_at = iota((depth, 128), 1)
    for head in range(2):
        col = jnp.sum(folded[:, head * DH : (head + 1) * DH] * pq_ref[head : head + 1, :], axis=1, keepdims=True)
        key_stage[head] = jnp.sum(jnp.where(lane_at == row_at + core * 16, col, 0.0), axis=0, keepdims=True)
    key_z[z * 2 + core] = key_stage[core]

    loads[2].wait()
    part = vw_ref[...].astype(f32)
    first_core = core == 0
    pieces = []
    for head in range(2):
        cuts = [part[:, head * VW + n * LANES : head * VW + (n + 1) * LANES] for n in range(VW // LANES)]
        cuts.append(jnp.zeros((HALF - depth * len(cuts), LANES), f32))
        pieces.append(jnp.concatenate(cuts, axis=0).astype(bf16))
    wbuf[z, y, core] = jnp.where(first_core, pieces[0], pieces[1])
    wstage[...] = jnp.where(first_core, pieces[1], pieces[0])

    loads[3].wait()
    starts_buf[block_at] = jnp.concatenate(
        [starts_ref[...].reshape(1, HALF), jnp.zeros((1, 128 - HALF), jnp.int32)], axis=1
    )

    pl.semaphore_wait(barrier, 3 * side - 1)

    def ref_of(buf, half, a, b):
        return buf.at[a, b, 0] if half == 0 else buf.at[b, a, 1]

    def dev_of(half, a, b):
        return at(a, b, core) if half == 0 else at(b, a, core)

    def own_of(half):
        return (z, y) if half == 0 else (y, z)

    def sem_of(sems, half, a, b):
        return sems.at[a, b, 0] if half == 0 else sems.at[b, a, 1]

    def ring(buf, recv, send, half, a, b, step):
        a0, b0 = own_of(half)
        ref = ref_of(buf, half, a, b)
        copy(
            ref, ref, send.at[half, 1], sem_of(recv, half, a, b), dev_of(half, a0, wrap(b0 + step))
        ).start()

    def pass_on(buf, recv, send, half, a, b, step, distance, even):
        last = distance == side // 2 - 1
        if not last or even == (step == 1):
            ring(buf, recv, send, half, a, b, step)

    def begin(buf, recv, send, half):
        a0, b0 = own_of(half)
        ref = ref_of(buf, half, a0, b0)
        for step in (1, -1):
            pass_on(buf, recv, send, half, a0, b0, step, 0, True)

        @pl.loop(1, side)
        def _(i):
            copy(
                ref, ref, send.at[half, 0], sem_of(recv, half, a0, b0), dev_of(half, wrap(a0 + i), b0)
            ).start()

    def visit(buf, recv, send, distance, t):
        for half in (0, 1):
            a0, b0 = own_of(half)
            for even, a in ((True, wrap(a0 - t)), (False, wrap(a0 + t + 1))):
                if distance == 0:

                    def take(half=half, a=a, b0=b0, even=even):
                        arrived(ref_of(buf, half, a, b0), sem_of(recv, half, a, b0))
                        for step in (1, -1):
                            pass_on(buf, recv, send, half, a, b0, step, 0, even)

                    if even:
                        pl.when(t > 0)(take)
                    else:
                        take()
                elif distance < side // 2:
                    for step in (1, -1):
                        b = wrap(b0 - step * distance)
                        arrived(ref_of(buf, half, a, b), sem_of(recv, half, a, b))
                        pass_on(buf, recv, send, half, a, b, step, distance, even)
                else:
                    b = wrap(b0 + distance)
                    arrived(ref_of(buf, half, a, b), sem_of(recv, half, a, b))

    def stage(buf, recv, send, distance):
        @pl.loop(0, side // 2)
        def _(t):
            visit(buf, recv, send, distance, t)

    def sent(buf, send):
        for half in (0, 1):
            ref = buf.at[0, pl.ds(0, side - 1), half]
            arrived(ref, send.at[half, 0])
            ref = buf.at[:, pl.ds(0, side - 1), half]
            arrived(ref, send.at[half, 1])

    weights = (wbuf, w_recv, w_send)
    sib_piece = wbuf.at[z, y, 1 - core]
    chips = side * side
    half_rows = 2 * HALF
    window = min(256, width)
    blocks = side * side * 2 * HALF // 128
    lefts = [min(4 * depth * b // 128 * 128, width - window) for b in range(blocks)]

    def send_keys():
        def keys_to(target, head):
            copy(key_stage.at[head], key_z.at[z * 2 + core], keyz_send, keyz_recv, target).start()

        @pl.loop(1, side)
        def _(i):
            for head in range(2):
                keys_to(at(wrap(z + i), y, head), head)

        keys_to(sibling, 1 - core)

    def send_piece():
        to_sibling[0].start()

    def send_bytes():
        loads[4].wait()
        to_sibling[1].start()

    def send_starts():
        for one in to_block:
            one.start()

    def begin_weights():
        @pl.when(first_core)
        def _():
            begin(*weights, 0)
            arrived(sib_piece, sib_recv.at[0])
            begin(*weights, 1)

        @pl.when(core == 1)
        def _():
            begin(*weights, 1)
            arrived(sib_piece, sib_recv.at[0])
            begin(*weights, 0)

    def norm_rows(ref, first, quarter):
        @pl.loop(quarter * rows // 128, (quarter + 1) * rows // 128)
        def _(i):
            at_row = pl.multiple_of(i * 32, 32)
            wide = ref[pl.ds(at_row, 32), :].astype(f32)
            scale = lax.rsqrt(jnp.mean(wide * wide, axis=-1, keepdims=True) + 1e-05)
            normed[pl.ds(pl.multiple_of(first + at_row, 32), 32), :] = (
                wide * scale * gain_ref[...].reshape(1, width)
            ).astype(bf16)

    def norm_own(quarter):
        if quarter == 0:
            loads[5].wait()
        norm_rows(bytes_ref, core * rows, quarter)

    def norm_sibling(quarter):
        if quarter == 0:
            arrived(sib_bytes, sib_recv.at[1])
        norm_rows(sib_bytes, (1 - core) * rows, quarter)

    def pass_keys():
        arrived(key_z.at[pl.ds(0, 2 * side - 1)], keyz_recv)
        key_y[y] = jnp.concatenate([key_z[2 * i] + key_z[2 * i + 1] for i in range(side)], axis=0)

        @pl.loop(1, side)
        def _(i):
            copy(key_y.at[y], key_y.at[y], keyy_send, keyy_recv, at(z, wrap(y + i), core)).start()

    def make_pick():
        column = iota((1, width), 1)
        column_chip = column // (2 * depth)
        column_row = lax.rem(column_chip, side) * side + column_chip // side
        pick_ref[...] = jnp.where(iota((chips, width), 0) == column_row, 1.0, 0.0).astype(bf16)
        column_lane = lax.rem(column // depth, 2) * 16 + lax.rem(column, depth)
        lane_row = iota((128, width), 0)
        lane_ref[...] = jnp.where(lax.rem(lane_row, 32) == column_lane, 1.0, 0.0)

    def make_member():
        for k in range(1, 4):
            other = lax.rem(block_at + k, 4)
            arrived(starts_buf.at[other], starts_recv.at[other])
        patch_sub = iota((HALF, 128), 0)
        patch_lane = iota((HALF, 128), 1)
        first_cols, next_cols = [], []
        for q in range(4):
            row = starts_buf[q]
            follow = (chip // 2 + 1) * (4 * rows) if q == 3 else starts_buf[q + 1][:, 0:1]
            row = jnp.where(iota((1, 128), 1) == HALF, follow, row)
            first_cols.append(jnp.sum(jnp.where(patch_lane == patch_sub, row, 0), axis=1, keepdims=True))
            next_cols.append(jnp.sum(jnp.where(patch_lane == patch_sub + 1, row, 0), axis=1, keepdims=True))
        first_col = jnp.concatenate(first_cols, axis=0)
        next_col = jnp.concatenate(next_cols, axis=0)
        position = chip * (2 * rows) + iota((1, 2 * rows), 1)
        member_ref[...] = jnp.where((first_col <= position) & (position < next_col), 1.0, 0.0)

    def make_choose():
        lane = iota((1, 128), 1)
        in_piece = lax.rem(lane, HALF)
        source = jnp.where(in_piece < 3 * depth, (lane // HALF) * depth + lax.rem(in_piece, depth), -100000)
        sub = iota((window, 128), 0)
        for b in range(blocks):
            choose_ref[b] = jnp.where(sub == source + (4 * depth * b - lefts[b]), 1.0, 0.0).astype(bf16)

    def pool():
        arrived(key_y.at[pl.ds(0, side - 1)], keyy_recv)
        table = key_y[...].reshape(chips, 128)
        high = table.astype(bf16).astype(f32)
        middle = (table - high).astype(bf16).astype(f32)
        low = (table - high - middle).astype(bf16).astype(f32)
        packed = (high + pltpu.roll(middle, 32, axis=1) + pltpu.roll(low, 64, axis=1)).astype(bf16)
        taken = dot(packed, pick_ref[...], ((0,), (0,)))
        key_rows = (taken * lane_ref[...]).astype(bf16)
        scores = jnp.sum(dot(key_rows, normed[...], ((1,), (1,))), axis=0, keepdims=True) / math.sqrt(DH)
        member = member_ref[...] > 0.5
        masked = jnp.where(member, scores, NEG)
        top = jnp.max(masked, axis=1, keepdims=True)
        weight = jnp.where(member, jnp.exp(masked - top), 0.0).astype(bf16)
        total = jnp.sum(weight.astype(f32), axis=1, keepdims=True)
        share = jnp.where(total > 0.0, 1.0 / jnp.maximum(total, 1e-30), 0.0)
        pooled_rows = dot(weight, normed[...]) * share
        own_rows[...] = pooled_rows.reshape(2, half_rows, width)
        send_rows[...] = pooled_rows.astype(bf16).reshape(2, half_rows, width)
        to_pair[0].start()
        eye = iota((4 * HALF, 128), 0) == iota((4 * HALF, 128), 1)
        top_row = jnp.sum(jnp.where(eye, top, 0.0), axis=0, keepdims=True)
        total_row = jnp.sum(jnp.where(eye, total, 0.0), axis=0, keepdims=True)
        send_stats[...] = jnp.concatenate([top_row, total_row, jnp.zeros((6, 128), f32)], axis=0)
        to_pair[1].start()

    def merge():
        to_pair[1].wait_recv()
        eye = iota((half_rows, 128), 1) == iota((half_rows, 128), 0) + pair_at * half_rows

        def to_column(row):
            return jnp.sum(jnp.where(eye, row, 0.0), axis=1, keepdims=True)

        own_top, own_total = to_column(send_stats[0:1, :]), to_column(send_stats[1:2, :])
        got_top, got_total = to_column(got_stats[0:1, :]), to_column(got_stats[1:2, :])
        top = jnp.maximum(own_top, got_top)
        own_part = jnp.exp(own_top - top) * own_total
        got_part = jnp.exp(got_top - top) * got_total
        share = 1.0 / (own_part + got_part)
        to_pair[0].wait_recv()
        merged = own_rows[pair_at] * (own_part * share) + got_rows[...].astype(f32) * (got_part * share)
        merged = merged.astype(bf16)
        which = lax.rem(iota((1, 128), 1), HALF) // depth
        for b in range(blocks):
            block = dot(merged[:, lefts[b] : lefts[b] + window], choose_ref[b])
            for n in range(3):
                spread[n * half_rows : (n + 1) * half_rows, b * 128 : (b + 1) * 128] = jnp.where(
                    which == n, block, 0.0
                ).astype(bf16)

    to_sibling = [
        copy(wstage, wbuf.at[z, y, core], sib_send.at[0], sib_recv.at[0], sibling),
        copy(bytes_ref, sib_bytes, sib_send.at[1], sib_recv.at[1], sibling),
    ]
    to_block = [
        copy(starts_buf.at[block_at], starts_buf.at[block_at], starts_send.at[k], starts_recv.at[block_at], target)
        for k, target in enumerate((sibling, pair, cross))
    ]
    to_pair = [
        copy(send_rows.at[1 - pair_at], got_rows, pair_send.at[0], pair_recv.at[0], pair),
        copy(send_stats, got_stats, pair_send.at[1], pair_recv.at[1], pair),
    ]
    send_keys()
    send_piece()
    send_starts()
    send_bytes()
    begin_weights()
    norm_own(0)
    norm_own(1)
    norm_own(2)
    norm_own(3)
    pass_keys()
    stage(*weights, 0)
    norm_sibling(0)
    norm_sibling(1)
    norm_sibling(2)
    norm_sibling(3)
    stage(*weights, 1)
    make_pick()
    make_member()
    stage(*weights, 2)
    pool()
    stage(*weights, 3)
    make_choose()
    stage(*weights, 4)
    merge()
    span = side * 2 * HALF

    def mapped(low, high):
        total = jnp.zeros(((high - low) * half_rows, LANES), f32)
        for zz in range(side):
            total = total + dot(
                spread[low * half_rows : high * half_rows, zz * span : (zz + 1) * span],
                wbuf[zz].reshape(span, LANES),
            )
        return total.astype(bf16)

    patches = (kvbuf, kv_recv, kv_send)
    kvbuf[z, y] = mapped(2, 3).reshape(2, HALF, LANES)
    begin(*patches, 0)
    begin(*patches, 1)
    mapped_queries = mapped(0, 2)
    queries = jnp.concatenate(
        [mapped_queries[n * half_rows : (n + 1) * half_rows, k * DH : (k + 1) * DH] for n in range(2) for k in range(2)],
        axis=0,
    )

    query_at = chip * half_rows + lax.rem(iota((1, GQ * half_rows), 1), half_rows)
    key_index = iota((side * HALF, 1), 0)
    top_ref[...] = jnp.full(top_ref.shape, NEG, f32)
    total_ref[...] = jnp.zeros(total_ref.shape, f32)
    mix_ref[...] = jnp.zeros(mix_ref.shape, f32)

    def attend(half, b):
        if half == 0:
            pair_of = kvbuf[:, b, 0]
            key_at = (key_index // HALF * side + b) * half_rows
        else:
            pair_of = kvbuf[b, :, 1]
            key_at = (key_index // HALF + b * side) * half_rows + HALF
        pair_of = pair_of.reshape(side * HALF, LANES)
        logits = dot(pair_of[:, :DH], queries, ((1,), (1,))) / math.sqrt(DH)
        logits = jnp.where(key_at + lax.rem(key_index, HALF) <= query_at, logits, NEG)
        old = top_ref[...]
        new = jnp.maximum(old, jnp.max(logits, axis=0, keepdims=True))
        raised = jnp.exp(logits - new)
        keep = jnp.exp(old - new)
        top_ref[...] = new
        total_ref[...] = total_ref[...] * keep + jnp.sum(raised, axis=0, keepdims=True)
        mix_ref[...] = mix_ref[...] * keep + dot(pair_of[:, DH:], raised.astype(bf16), ((0,), (0,)))

    def ready_at(distance):
        for half in (0, 1):
            b0 = own_of(half)[1]
            if distance == 0:
                yield half, b0
            elif distance == side // 2:
                yield half, wrap(b0 + distance)
            else:
                yield half, wrap(b0 + distance)
                yield half, wrap(b0 - distance)

    queue = []
    for distance in range(side // 2 + 1):
        for t in range(side // 2):
            visit(*patches, distance, t)
            if queue:
                attend(*queue.pop(0))
        queue += list(ready_at(distance))
    for one in queue:
        attend(*one)

    mixed = (mix_ref[...] / total_ref[...]).T
    mixed = jnp.concatenate([mixed[h * half_rows : (h + 1) * half_rows] for h in range(GQ)], axis=1).astype(bf16)
    own_out = jnp.where(first_core, mixed[:HALF], mixed[HALF:])
    out_send[...] = jnp.where(first_core, mixed[HALF:], mixed[:HALF])
    last = copy(out_send, out_got, out_send_sem, out_recv, sibling)
    last.start()
    for one in to_sibling + to_block + to_pair:
        one.wait_send()
    arrived(key_z.at[pl.ds(0, 2 * side - 1)], keyz_send)
    arrived(key_y.at[pl.ds(0, side - 1)], keyy_send)
    sent(wbuf, w_send)
    sent(kvbuf, kv_send)
    last.wait()
    theirs = out_got[...]
    out_ref[:, : GQ * DH] = jnp.where(first_core, own_out, theirs)
    out_ref[:, GQ * DH :] = jnp.where(first_core, theirs, own_out)


def on_device(seq, byte_rows, norm_gain, key_weight, value_weight, pool_query, patch_starts):
    side = math.isqrt(seq // 2)
    rows, width = byte_rows.shape
    gathered = (side, side, 2, HALF, LANES)
    dma = pltpu.SemaphoreType.DMA
    scratch = [
        pltpu.VMEM((rows, width), bf16),
        pltpu.VMEM(norm_gain.shape, f32),
        pltpu.VMEM(key_weight.shape, bf16),
        pltpu.VMEM(value_weight.shape, bf16),
        pltpu.VMEM(pool_query.shape, f32),
        pltpu.VMEM(patch_starts.shape, jnp.int32),
        pltpu.VMEM(gathered, bf16),
        pltpu.VMEM(gathered, bf16),
        pltpu.VMEM((HALF, LANES), bf16),
        pltpu.VMEM((rows, width), bf16),
        pltpu.VMEM((2 * rows, width), bf16),
        pltpu.VMEM((4, 1, 128), jnp.int32),
        pltpu.VMEM((2, 1, 128), f32),
        pltpu.VMEM((2 * side, 1, 128), f32),
        pltpu.VMEM((side, side, 128), f32),
        pltpu.VMEM((2, 2 * HALF, width), bf16),
        pltpu.VMEM((2, 2 * HALF, width), f32),
        pltpu.VMEM((2 * HALF, width), bf16),
        pltpu.VMEM((8, 128), f32),
        pltpu.VMEM((8, 128), f32),
        pltpu.VMEM((6 * HALF, side * side * 2 * HALF), bf16),
        pltpu.VMEM((side * side, width), bf16),
        pltpu.VMEM((128, width), f32),
        pltpu.VMEM((4 * HALF, 2 * rows), f32),
        pltpu.VMEM((side * side * 2 * HALF // 128, min(256, width), 128), bf16),
        pltpu.VMEM((1, 2 * HALF * GQ), f32),
        pltpu.VMEM((1, 2 * HALF * GQ), f32),
        pltpu.VMEM((DH, 2 * HALF * GQ), f32),
        pltpu.VMEM((HALF, GQ * DH), bf16),
        pltpu.VMEM((HALF, GQ * DH), bf16),
        dma((6,)),
        dma((side, side, 2)),
        dma((side, side, 2)),
        dma((2,)),
        dma((4,)),
        dma(()),
        dma(()),
        dma((2,)),
        dma(()),
        dma((2, 2)),
        dma((2, 2)),
        dma((2,)),
        dma((3,)),
        dma(()),
        dma(()),
        dma((2,)),
        dma(()),
    ]
    return pl.pallas_call(
        functools.partial(kernel, side),
        out_shape=jax.ShapeDtypeStruct((HALF, 2 * GQ * DH), bf16),
        in_specs=[pl.BlockSpec(memory_space=pl.ANY)] * 6,
        out_specs=pl.BlockSpec(memory_space=pltpu.VMEM),
        scratch_shapes=scratch,
        compiler_params=pltpu.CompilerParams(
            collective_id=0, has_side_effects=True, vmem_limit_bytes=60 * 1024 * 1024
        ),
    )(byte_rows, norm_gain, key_weight, value_weight, pool_query, patch_starts)


def solution(mesh):
    return jax.shard_map(
        functools.partial(on_device, mesh.shape["seq"]),
        mesh=mesh,
        in_specs=(
            P(("dp", "seq"), None),
            P(),
            P("seq", "mp"),
            P("seq", "mp"),
            P("mp", None),
            P(("dp", "seq")),
        ),
        out_specs=P(("dp", "seq"), "mp"),
        check_vma=False,
    )
```

time: 71.3 us -> 65.1 us (0.913)
  Pallas kernels: 67.7 us -> 63.4 us
  local copies, waits for them, and re-layouts: 3.26 us -> 1.47 us
    pallas_call x1, Pallas kernels: 67.7 us -> 63.4 us  [on_device(): pl.pallas_call(functools.partial(kernel, side), out_shape=jax.ShapeDtypeS...]
    unnamed x11 -> x1, local copies, waits for them, and re-layouts: 2.52 us -> 1.47 us
    reshape x1 -> x0, local copies, waits for them, and re-layouts: 0.74 us -> none  [on_device(): norm_gain.reshape(1, width)]
where the time goes in v2:
time: 65.1 us; the launch traced here: 64.9 us
  Pallas kernels  63.4 us (97%)
  local copies, waits for them, and re-layouts  1.47 us (2%)
    pallas_call x1, Pallas kernels, on_device(): pl.pallas_call(functools.partial(kernel, side), out_shape=jax.ShapeDtypeS...  63.4 us
    unnamed x1, local copies, waits for them, and re-layouts  1.47 us

profile of v2, /device:TPU:1, one launch (start us, length us, event | category | flops | bytes accessed | tf_op | source)
XLA Modules:
  0.0 64.9 jit_solution(16524029456827988510)
XLA Ops:
  0.0 63.4 %shard_map.64 = bf16[32,1024]{1,0:T(8,128)(2,1)} custom-call(bf16[256,1280]{1,0:T(8,128)(2,1)} %bytes_in.1, f32[1280]{0:T(1024)} %gain_in.1, bf16[10,256]{1,0:T(8,128)(2,1)} %kw_in.1, bf16[10,1536]{1,0:T(8,128)(2,1)} %vw_in.1, f32[2,128]{1,0:T(2,128)} %pq_in.1, s32[32]{0:T(128)} %starts_in.1), custom_call_target="tpu_custom_call" | custom-call | tf_op jit(solution)/shard_map/pallas_call | solution.py:582
  63.4 1.5 %copy.8 = bf16[32,1024]{1,0:T(8,128)(2,1)} copy(bf16[32,1024]{1,0:T(8,128)(2,1)} %shard_map.64) | data formatting | bytes 131072

commit v3 on v2

--- a/solution.py
+++ b/solution.py
@@ -61,6 +61,7 @@
     lane_ref,
     member_ref,
     choose_ref,
+    score_ref,
     top_ref,
     total_ref,
     mix_ref,
@@ -213,8 +214,8 @@
                 ref, ref, send.at[half, 0], sem_of(recv, half, a0, b0), dev_of(half, wrap(a0 + i), b0)
             ).start()
 
-    def visit(buf, recv, send, distance, t):
-        for half in (0, 1):
+    def visit(buf, recv, send, distance, t, halves=(0, 1)):
+        for half in halves:
             a0, b0 = own_of(half)
             for even, a in ((True, wrap(a0 - t)), (False, wrap(a0 + t + 1))):
                 if distance == 0:
@@ -355,7 +356,7 @@
         for b in range(blocks):
             choose_ref[b] = jnp.where(sub == source + (4 * depth * b - lefts[b]), 1.0, 0.0).astype(bf16)
 
-    def pool():
+    def score():
         arrived(key_y.at[pl.ds(0, side - 1)], keyy_recv)
         table = key_y[...].reshape(chips, 128)
         high = table.astype(bf16).astype(f32)
@@ -364,9 +365,11 @@
         packed = (high + pltpu.roll(middle, 32, axis=1) + pltpu.roll(low, 64, axis=1)).astype(bf16)
         taken = dot(packed, pick_ref[...], ((0,), (0,)))
         key_rows = (taken * lane_ref[...]).astype(bf16)
-        scores = jnp.sum(dot(key_rows, normed[...], ((1,), (1,))), axis=0, keepdims=True) / math.sqrt(DH)
+        score_ref[...] = jnp.sum(dot(key_rows, normed[...], ((1,), (1,))), axis=0, keepdims=True) / math.sqrt(DH)
+
+    def pool():
         member = member_ref[...] > 0.5
-        masked = jnp.where(member, scores, NEG)
+        masked = jnp.where(member, score_ref[...], NEG)
         top = jnp.max(masked, axis=1, keepdims=True)
         weight = jnp.where(member, jnp.exp(masked - top), 0.0).astype(bf16)
         total = jnp.sum(weight.astype(f32), axis=1, keepdims=True)
@@ -435,12 +438,16 @@
     stage(*weights, 1)
     make_pick()
     make_member()
-    stage(*weights, 2)
+    visit(*weights, 2, 0)
+    visit(*weights, 2, 1)
+    score()
+    visit(*weights, 2, 2)
+    visit(*weights, 2, 3)
     pool()
     stage(*weights, 3)
     make_choose()
+    merge()
     stage(*weights, 4)
-    merge()
     span = side * 2 * HALF
 
     def mapped(low, high):
@@ -491,21 +498,23 @@
             b0 = own_of(half)[1]
             if distance == 0:
                 yield half, b0
-            elif distance == side // 2:
-                yield half, wrap(b0 + distance)
             else:
                 yield half, wrap(b0 + distance)
                 yield half, wrap(b0 - distance)
 
     queue = []
-    for distance in range(side // 2 + 1):
+    for distance in range(side // 2):
         for t in range(side // 2):
             visit(*patches, distance, t)
             if queue:
                 attend(*queue.pop(0))
         queue += list(ready_at(distance))
-    for one in queue:
-        attend(*one)
+    for half in (0, 1):
+        for t in range(side // 2):
+            visit(*patches, side // 2, t, (half,))
+            if queue:
+                attend(*queue.pop(0))
+        attend(half, wrap(own_of(half)[1] + side // 2))
 
     mixed = (mix_ref[...] / total_ref[...]).T
     mixed = jnp.concatenate([mixed[h * half_rows : (h + 1) * half_rows] for h in range(GQ)], axis=1).astype(bf16)
@@ -556,6 +565,7 @@
         pltpu.VMEM((128, width), f32),
         pltpu.VMEM((4 * HALF, 2 * rows), f32),
         pltpu.VMEM((side * side * 2 * HALF // 128, min(256, width), 128), bf16),
+        pltpu.VMEM((1, 2 * rows), f32),
         pltpu.VMEM((1, 2 * HALF * GQ), f32),
         pltpu.VMEM((1, 2 * HALF * GQ), f32),
         pltpu.VMEM((DH, 2 * HALF * GQ), f32),

time: 65.1 us -> 64.5 us (level)
  no operation moved by 1% of the time
where the time goes in v3:
time: 64.5 us; the launch traced here: 64.3 us
  Pallas kernels  62.8 us (97%)
  local copies, waits for them, and re-layouts  1.47 us (2%)
    pallas_call x1, Pallas kernels, on_device(): pl.pallas_call(functools.partial(kernel, side), out_shape=jax.ShapeDtypeS...  62.8 us
    unnamed x1, local copies, waits for them, and re-layouts  1.47 us

profile of v3, /device:TPU:1, one launch (start us, length us, event | category | flops | bytes accessed | tf_op | source)
XLA Modules:
  0.0 64.3 jit_solution(2056369565223949686)
XLA Ops:
  0.0 62.8 %shard_map.64 = bf16[32,1024]{1,0:T(8,128)(2,1)} custom-call(bf16[256,1280]{1,0:T(8,128)(2,1)} %bytes_in.1, f32[1280]{0:T(1024)} %gain_in.1, bf16[10,256]{1,0:T(8,128)(2,1)} %kw_in.1, bf16[10,1536]{1,0:T(8,128)(2,1)} %vw_in.1, f32[2,128]{1,0:T(2,128)} %pq_in.1, s32[32]{0:T(128)} %starts_in.1), custom_call_target="tpu_custom_call" | custom-call | tf_op jit(solution)/shard_map/pallas_call | solution.py:592
  62.8 1.5 %copy.8 = bf16[32,1024]{1,0:T(8,128)(2,1)} copy(bf16[32,1024]{1,0:T(8,128)(2,1)} %shard_map.64) | data formatting | bytes 131072

commit v4 on v3

--- a/solution.py
+++ b/solution.py
@@ -596,7 +596,7 @@
         out_specs=pl.BlockSpec(memory_space=pltpu.VMEM),
         scratch_shapes=scratch,
         compiler_params=pltpu.CompilerParams(
-            collective_id=0, has_side_effects=True, vmem_limit_bytes=60 * 1024 * 1024
+            collective_id=0, has_side_effects=True, vmem_limit_bytes=54800 * 1024
         ),
     )(byte_rows, norm_gain, key_weight, value_weight, pool_query, patch_starts)
 

time: 64.5 us -> 66.7 us (1.034)
  local copies, waits for them, and re-layouts: 1.47 us -> 4.16 us
    unnamed x1 -> x11, local copies, waits for them, and re-layouts: 1.47 us -> 4.16 us
where the time goes in v4:
time: 66.7 us; the launch traced here: 66.5 us
  Pallas kernels  62.3 us (93%)
  local copies, waits for them, and re-layouts  4.16 us (6%)
    pallas_call x1, Pallas kernels, on_device(): pl.pallas_call(functools.partial(kernel, side), out_shape=jax.ShapeDtypeS...  62.3 us
    unnamed x11, local copies, waits for them, and re-layouts  4.16 us

profile of v4, /device:TPU:1, one launch (start us, length us, event | category | flops | bytes accessed | tf_op | source)
XLA Modules:
  0.0 66.5 jit_solution(6957593234382574618)
XLA Ops:
  0.0 0.0 copy-start
  0.0 0.8 %copy-done = bf16[10,1536]{1,0:T(8,128)(2,1)S(1)} copy-done((bf16[10,1536]{1,0:T(8,128)(2,1)S(1)}, bf16[10,1536]{1,0:T(8,128)(2,1)}, u32[]{:S(2)}) %copy-start) | copy-done | bytes 30744
  0.8 0.0 copy-start.1
  0.8 0.7 %copy-done.1 = f32[1280]{0:T(1024)S(1)} copy-done((f32[1280]{0:T(1024)S(1)}, f32[1280]{0:T(1024)}, u32[]{:S(2)}) %copy-start.1) | copy-done | bytes 5144
  1.5 0.0 copy-start.2
  1.5 0.7 %copy-done.2 = bf16[10,256]{1,0:T(8,128)(2,1)S(1)} copy-done((bf16[10,256]{1,0:T(8,128)(2,1)S(1)}, bf16[10,256]{1,0:T(8,128)(2,1)}, u32[]{:S(2)}) %copy-start.2) | copy-done | bytes 5144
  2.2 0.0 copy-start.3
  2.2 0.7 %copy-done.3 = f32[2,128]{1,0:T(2,128)S(1)} copy-done((f32[2,128]{1,0:T(2,128)S(1)}, f32[2,128]{1,0:T(2,128)}, u32[]{:S(2)}) %copy-start.3) | copy-done | bytes 1048
  2.9 0.0 copy-start.4
  2.9 0.7 copy-done.4
  3.5 62.3 %shard_map.64 = bf16[32,1024]{1,0:T(8,128)(2,1)S(1)} custom-call(bf16[256,1280]{1,0:T(8,128)(2,1)} %bytes_in.1, f32[1280]{0:T(1024)S(1)} %copy-done.1, bf16[10,256]{1,0:T(8,128)(2,1)S(1)} %copy-done.2, bf16[10,1536]{1,0:T(8,128)(2,1)S(1)} %copy-done, f32[2,128]{1,0:T(2,128)S(1)} %copy-done.3, s32[32]{0:T(128)S(1)} %copy-done.4), custom_call_target="tpu_custom_call" | custom-call | tf_op jit(solution)/shard_map/pallas_call | solution.py:592
  65.8 0.6 copy.8
Async XLA Ops:
  0.0 0.8 %copy-start = (bf16[10,1536]{1,0:T(8,128)(2,1)S(1)}, bf16[10,1536]{1,0:T(8,128)(2,1)}, u32[]{:S(2)}) copy-start(bf16[10,1536]{1,0:T(8,128)(2,1)} %vw_in.1) | copy-start | bytes 92164
  0.8 0.7 %copy-start.1 = (f32[1280]{0:T(1024)S(1)}, f32[1280]{0:T(1024)}, u32[]{:S(2)}) copy-start(f32[1280]{0:T(1024)} %gain_in.1) | copy-start | bytes 15364
  1.5 0.7 %copy-start.2 = (bf16[10,256]{1,0:T(8,128)(2,1)S(1)}, bf16[10,256]{1,0:T(8,128)(2,1)}, u32[]{:S(2)}) copy-start(bf16[10,256]{1,0:T(8,128)(2,1)} %kw_in.1) | copy-start | bytes 15364
  2.2 0.7 %copy-start.3 = (f32[2,128]{1,0:T(2,128)S(1)}, f32[2,128]{1,0:T(2,128)}, u32[]{:S(2)}) copy-start(f32[2,128]{1,0:T(2,128)} %pq_in.1) | copy-start | bytes 3076
  2.9 0.7 copy-start.4
